TPU v7x, 32 devices: a whole 2x2x4 slice. The times are simulated.
32 devices in a mesh: lat: 8 (over y, x, core), lon: 4 (over z).
Axes of the slice: x: 2, y: 2, z: 4, core: 2. Of those that a mesh axis runs over, the one named last changes fastest.
Arguments:
- tracer: float32 [32, 256, 2048], P(None, 'lat', 'lon'), may hold values from -6 to 6
- source: int32 [256, 16], P('lat', 'lon'), may hold values from 0 to 4095, as said below
- offset: int32 [256, 2048], P('lat', 'lon'), may hold values from 1 to 125
- fraction: float32 [256, 2048], P('lat', 'lon'), may hold values from 0 to 1
- cutoffs: int32 [2, 8], replicated, may hold values from 2 to 255
Outputs:
- advected: float32 [32, 256, 2048], P(None, 'lat', 'lon')
Inputs may be any that keep to these rules, and one draw needn't show every extreme that they name: With source[j, b] = rho * 16 + beta: |rho - j| <= 2, and some arrival blocks reach 2 in both directions. Rows j with 8 <= j < 248 have beta equal to b - 1, b or b + 1 modulo 16. Rows within 8 of a pole have rho within the same band of 8 rows at that pole and beta anywhere on the circle.
All inputs are finite; a program needn't handle non-finite values.
Results may differ from a plain program's by a relative error of at most 0.000071.
Values sent between devices are 32-bit elements; how exact they have to be, the bound alone decides.
A program may use at most 128 MiB of HBM per device.

v0:
```python
import math

import jax
import jax.numpy as jnp
from jax import lax
from jax.sharding import PartitionSpec as P

NLON = 2048
BLK = 128
HL = 2
PROWS = 8


def extended(cells, sides, width, closed):
    for axis, dim in sides:
        count = lax.axis_size(axis)
        ends = count if closed else count - 1
        head = lax.slice_in_dim(cells, 0, width, axis=dim)
        tail = lax.slice_in_dim(cells, cells.shape[dim] - width, cells.shape[dim], axis=dim)
        cells = jnp.concatenate(
            [
                lax.ppermute(tail, axis, [(i, (i + 1) % count) for i in range(ends)]),
                cells,
                lax.ppermute(head, axis, [((i + 1) % count, i) for i in range(ends)]),
            ],
            axis=dim,
        )
    return cells


def cubic_limited(before_one, at_anchor, after_one, after_two, position):
    weight_before = -position * (position - 1.0) * (position - 2.0) / 6.0
    weight_anchor = (position + 1.0) * (position - 1.0) * (position - 2.0) / 2.0
    weight_after = -(position + 1.0) * position * (position - 2.0) / 2.0
    weight_beyond = (position + 1.0) * position * (position - 1.0) / 6.0
    interpolated = (
        weight_before * before_one
        + weight_anchor * at_anchor
        + weight_after * after_one
        + weight_beyond * after_two
    )
    lowest_bound = jnp.minimum(at_anchor, after_one)
    upper_bound = jnp.maximum(at_anchor, after_one)
    return jnp.minimum(jnp.maximum(interpolated, lowest_bound), upper_bound)


def spectral_table(first_cell, cell_total):
    cell_ids = first_cell + jnp.arange(cell_total, dtype=jnp.int32)
    wavenumbers = jnp.arange(NLON // 2, dtype=jnp.int32)
    phases = cell_ids[:, None] * wavenumbers[None, :] % NLON
    angles = phases.astype(jnp.float32) * (2.0 * math.pi / NLON)
    return jnp.concatenate([jnp.cos(angles), jnp.sin(angles)], axis=1)


def damping_rows(cutoff_values):
    wavenumbers = jnp.arange(NLON // 2, dtype=jnp.int32)
    ratios = cutoff_values.astype(jnp.float32)[..., None] / jnp.maximum(wavenumbers, 1).astype(
        jnp.float32
    )
    half_weights = jnp.where(wavenumbers >= 1, jnp.maximum(1.0 - ratios, 0.0), 0.0) * (2.0 / NLON)
    return jnp.concatenate([half_weights, half_weights], axis=-1)


def take_cells(values, indices):
    return jnp.take(values, indices, axis=1)


def polar_work(slab_data, source_rows, source_cells, positions, cutoff_rows, first_cell, lon_width):
    pole_count = slab_data.shape[0]
    channel_count = slab_data.shape[1]
    cell_span = PROWS * lon_width
    flat_rows = source_rows.reshape(pole_count, cell_span)
    flat_cells = source_cells.reshape(pole_count, cell_span)
    zeros_init = jnp.zeros((pole_count, channel_count, cell_span), jnp.float32)
    totals = (zeros_init, zeros_init, zeros_init, zeros_init)
    portion = lax.all_gather(slab_data, "lon", axis=3, tiled=True)
    length = portion.shape[3]
    flat_portion = portion.reshape(pole_count, channel_count, PROWS * length)
    results = []
    for step_offset, partial_sum in zip((-1, 0, 1, 2), totals):
        column = flat_cells + step_offset
        inside = (column >= 0) & (column < length)
        gather_index = flat_rows * length + jnp.clip(column, 0, length - 1)
        picked = jax.vmap(take_cells)(flat_portion, gather_index)
        results.append(jnp.where(inside[:, None, :], picked, 0.0))
    before_one, at_anchor, after_one, after_two = tuple(results)
    limited = cubic_limited(
        before_one, at_anchor, after_one, after_two, positions.reshape(pole_count, 1, cell_span)
    )
    shaped = limited.reshape(pole_count, channel_count, PROWS, lon_width)
    fourier_basis = spectral_table(first_cell, lon_width)
    spectra = jnp.einsum("pcrx,xk->pcrk", shaped, fourier_basis, precision=lax.Precision.HIGHEST)
    spectra = lax.psum(spectra, "lon")
    weights = damping_rows(cutoff_rows)
    removed = jnp.einsum(
        "pcrk,xk->pcrx", spectra * weights[:, None], fourier_basis, precision=lax.Precision.HIGHEST
    )
    return shaped - removed


def body(tracer, source, offset, fraction, cutoffs):
    channels, lat_rows, lon_cells = tracer.shape
    lat_count = lax.axis_size("lat")
    lat_place = lax.axis_index("lat")
    lon_place = lax.axis_index("lon")
    first_row = lat_place * lat_rows
    first_cell = lon_place * lon_cells
    all_rows = lat_rows * lat_count
    block_count = NLON // BLK
    cell_block = jnp.arange(lon_cells, dtype=jnp.int32) // BLK
    per_cell = jnp.take(source, cell_block, axis=1)
    source_row = per_cell // block_count
    source_block = per_cell % block_count
    padded_rows = extended(tracer, (("lat", 1),), HL, False)
    widened = extended(padded_rows, (("lon", 2),), BLK, True)
    row_total = lat_rows + 2 * HL
    width_total = lon_cells + 2 * BLK
    local_row = jnp.clip(source_row - first_row + HL, 0, row_total - 1)
    local_start = jnp.clip(
        jnp.mod(source_block * BLK - first_cell + BLK, NLON), 0, width_total - BLK
    )
    anchor = local_row * width_total + local_start + offset
    flat_field = widened.reshape(channels, row_total * width_total)

    def stencil(shift_by):
        return jnp.take(flat_field, (anchor + shift_by).reshape(-1), axis=1).reshape(
            channels, lat_rows, lon_cells
        )

    limited = cubic_limited(stencil(-1), stencil(0), stencil(1), stencil(2), fraction[None])
    slab_first = jnp.where(lat_place == 0, 0, lat_rows - PROWS).astype(jnp.int32)
    slab_global = first_row + slab_first
    pole_side = jnp.where(lat_place == 0, 0, 1).astype(jnp.int32)

    def rows_of(values):
        return lax.dynamic_slice_in_dim(values, slab_first, PROWS, 0)

    slab_rows = jnp.clip(rows_of(source_row) - slab_global, 0, PROWS - 1)
    slab_cells = rows_of(source_block * BLK + offset)
    slab_fraction = rows_of(fraction)
    slab_tracer = lax.dynamic_slice_in_dim(tracer, slab_first, PROWS, 1)
    cutoff_rows = lax.dynamic_slice_in_dim(cutoffs, pole_side, 1, 0)
    filtered = polar_work(
        slab_tracer[None],
        slab_rows[None],
        slab_cells[None],
        slab_fraction[None],
        cutoff_rows,
        first_cell,
        lon_cells,
    )
    polar_result = filtered.reshape(channels, PROWS, lon_cells)
    updated = lax.dynamic_update_slice_in_dim(limited, polar_result, slab_first, 1)
    global_rows = first_row + jnp.arange(lat_rows, dtype=jnp.int32)
    polar_mask = (global_rows < PROWS) | (global_rows >= all_rows - PROWS)
    return jnp.where(polar_mask[None, :, None], updated, limited)


def solution(mesh):
    placed = (P(None, "lat", "lon"), P("lat", "lon"), P("lat", "lon"), P("lat", "lon"), P())
    return jax.shard_map(
        body, mesh=mesh, in_specs=placed, out_specs=P(None, "lat", "lon"), check_vma=False
    )
```

profile of v0, /device:TPU:0, one launch (start us, length us, event | category | flops | bytes accessed | tf_op | source)
XLA Modules:
  0.0 735.4 jit_solution(9071469983450961483)
XLA Ops:
  7.9 2.4 collective-permute-start
  18.0 9.6 %fusion.22 = (f32[512,1024]{1,0:T(8,128)S(1)}, f32[512,1024]{1,0:T(8,128)}) fusion(s32[512]{0:T(512)S(1)} %iota_add_fusion), kind=kLoop, calls=%fused_computation.35 | loop fusion | flops 7340032 | bytes 4196352 | tf_op jit(solution)/shard_map/cos | solution.py:52
  27.8 2.8 constant_dynamic-update-slice_fusion.1
  30.8 4.5 collective-permute-start.3
  38.5 45.2 %collective-permute-done.3 = f32[32,36,128]{2,0,1:T(8,128)S(1)} collective-permute-done((f32[32,36,128]{2,0,1:T(8,128)S(1)}, f32[32,36,128]{2,0,1:T(8,128)S(1)}, u32[]{:S(2)}, u32[]{:S(2)}) %collective-permute-start.3) | collective-permute-done | bytes 589856 | tf_op jit(solution)/shard_map/ppermute | solution.py:24
  83.8 3.6 collective-permute-done.2
  89.5 8.9 %copy.64 = f32[32,36,768]{0,2,1:T(8,128)} copy(f32[32,36,768]{2,0,1:T(8,128)} %pad_maximum_fusion) | data formatting | bytes 7077888 | tf_op jit(solution)/shard_map/concatenate | solution.py:20
  98.4 59.5 %gather_fusion.2 = f32[16384,32]{1,0:T(8,128)} fusion(f32[32,27648]{0,1:T(8,128)} %bitcast.182, s32[16384]{0:T(1024)S(1)} %fusion.49), kind=kCustom, calls=%fused_computation.2.clone | custom fusion | bytes 4259840 | tf_op jit(solution)/shard_map/jit(_take)/gather | solution.py:126
  157.9 59.5 %gather_fusion.3 = f32[16384,32]{1,0:T(8,128)} fusion(f32[32,27648]{0,1:T(8,128)} %bitcast.183, s32[16384]{0:T(1024)S(1)} %fusion.50), kind=kCustom, calls=%fused_computation.3.clone | custom fusion | bytes 4259840 | tf_op jit(solution)/shard_map/jit(_take)/gather | solution.py:126
  217.4 59.5 %gather_fusion.4 = f32[16384,32]{1,0:T(8,128)} fusion(f32[32,27648]{0,1:T(8,128)} %bitcast.184, s32[16384]{0:T(1024)S(1)} %fusion.51), kind=kCustom, calls=%fused_computation.4.clone | custom fusion | bytes 4259840 | tf_op jit(solution)/shard_map/jit(_take)/gather | solution.py:126
  276.9 59.5 %gather_fusion.1 = f32[16384,32]{1,0:T(8,128)} fusion(f32[32,27648]{0,1:T(8,128)} %bitcast.185, s32[16384]{0:T(1024)S(1)} %fusion.48), kind=kCustom, calls=%fused_computation.clone | custom fusion | bytes 4259840 | tf_op jit(solution)/shard_map/jit(_take)/gather | solution.py:126
  336.4 14.3 %broadcast_select_fusion.2 = f32[16384,32]{1,0:T(8,128)} fusion(f32[16384,32]{1,0:T(8,128)} %gather_fusion.2, pred[16384]{0:T(1024)(128)(4,1)S(1)} %compare_and_fusion.2), kind=kLoop, calls=%fused_computation.12 | loop fusion | flops 524288 | bytes 4210688 | tf_op jit(solution)/shard_map/jit(_take)/select_n | solution.py:126
  350.7 10.2 %broadcast_select_fusion.1 = f32[16384,32]{1,0:T(8,128)} fusion(f32[16384,32]{1,0:T(8,128)S(1)} %copy-done.3, pred[16384]{0:T(1024)(128)(4,1)S(1)} %compare_and_fusion.1), kind=kLoop, calls=%fused_computation.11 | loop fusion | flops 524288 | bytes 4210688 | tf_op jit(solution)/shard_map/jit(_take)/select_n | solution.py:126
  360.9 10.1 %broadcast_select_fusion = f32[16384,32]{1,0:T(8,128)} fusion(f32[16384,32]{1,0:T(8,128)S(1)} %bitcast.199, pred[16384]{0:T(1024)(128)(4,1)S(1)} %copy-done.7), kind=kLoop, calls=%fused_computation.10 | loop fusion | flops 524288 | bytes 4210688 | tf_op jit(solution)/shard_map/jit(_take)/select_n | solution.py:126
  371.0 6.3 copy.69
  377.3 59.8 %gather_fusion.8 = f32[4096,32]{1,0:T(8,128)} fusion(f32[1,32,16384]{1,2,0:T(8,128)} %bitcast.190, s32[4096]{0:T(1024)S(1)} %bitcast.186), kind=kCustom, calls=%fused_computation.7.clone | custom fusion | bytes 1081344 | tf_op jit(solution)/shard_map/vmap(jit(_take))/gather | solution.py:65
  437.1 2.2 copy.73
  439.2 59.9 %gather_fusion.5 = f32[4096,32]{1,0:T(8,128)} fusion(f32[1,32,16384]{1,2,0:T(8,128)} %bitcast.191, s32[4096]{0:T(1024)S(1)} %bitcast.187), kind=kCustom, calls=%fused_computation.1.clone | custom fusion | bytes 1081344 | tf_op jit(solution)/shard_map/vmap(jit(_take))/gather | solution.py:65
  499.2 2.2 copy.70
  501.3 59.9 %gather_fusion.7 = f32[4096,32]{1,0:T(8,128)} fusion(f32[1,32,16384]{1,2,0:T(8,128)} %bitcast.192, s32[4096]{0:T(1024)S(1)} %bitcast.188), kind=kCustom, calls=%fused_computation.6.clone | custom fusion | bytes 1081344 | tf_op jit(solution)/shard_map/vmap(jit(_take))/gather | solution.py:65
  561.2 3.0 copy.72
  564.3 60.0 %gather_fusion.6 = f32[4096,32]{1,0:T(8,128)} fusion(f32[1,32,16384]{1,2,0:T(8,128)} %bitcast.193, s32[4096]{0:T(1024)S(1)} %bitcast.189), kind=kCustom, calls=%fused_computation.5.clone | custom fusion | bytes 1081344 | tf_op jit(solution)/shard_map/vmap(jit(_take))/gather | solution.py:65
  624.3 3.0 copy.71
  629.5 5.0 fusion.2
  635.3 13.1 %broadcast_select_fusion.3 = f32[16384,32]{1,0:T(8,128)} fusion(f32[16384,32]{1,0:T(8,128)} %gather_fusion.1, pred[16384]{0:T(1024)(128)(4,1)S(1)} %copy-done.6), kind=kLoop, calls=%fused_computation.13 | loop fusion | flops 524288 | bytes 4210688 | tf_op jit(solution)/shard_map/jit(_take)/select_n | solution.py:126
  648.4 6.4 copy.75
  654.8 6.5 copy.76
  661.3 6.5 copy.77
  667.8 6.5 copy.74
  674.3 6.1 maximum_minimum_fusion
  680.4 41.3 %all-reduce.2.cloned.1.call-done = f32[1,32,8,2048]{3,2,1,0:T(8,128)} async-done(((f32[1,32,8,2048]{3,2,1,0:T(8,128)}), f32[1,32,8,2048]{3,2,1,0:T(8,128)}) %all-reduce.2.cloned.1.call-update) | async-done | bytes 2097168 | tf_op jit(solution)/shard_map/psum | solution.py:93
  721.7 6.9 fusion.17
  (108 shorter events, 17.3 us)
Async XLA Ops:
  6.5 7.2 copy-start
  6.5 8.4 %copy-start.5 = (s32[32,512]{1,0:T(8,128)S(1)}, s32[32,512]{1,0:T(8,128)}, u32[]{:S(2)}) copy-start(s32[32,512]{1,0:T(8,128)} %param.11) | copy-start | bytes 196612
  6.5 364.5 %all-gather.3.cloned.1.call-start = ((), (), s32[]{:S(2)}) async-start(), calls=%async_computation.1 | async-start | bytes 2621440 | tf_op jit(solution)/shard_map/all_gather | solution.py:76
  7.9 19.9 %collective-permute-start = (f32[32,2,512]{2,0,1:T(8,128)S(1)}, f32[32,2,512]{2,0,1:T(8,128)S(1)}, u32[]{:S(2)}, u32[]{:S(2)}) collective-permute-start(f32[32,2,512]{2,0,1:T(8,128)S(1)} %copy.93), channel_id=1, source_target_pairs={{0,4},{4,8},{8,12},{12,16},{16,20},{20,24},{24,28},{1,5},{5,9},{9,... | collective-permute-start | bytes 393224 | tf_op jit(solution)/shard_map/ppermute | solution.py:22
  10.3 5.6 copy-start.4
  10.3 20.3 %collective-permute-start.1 = (f32[32,2,512]{2,0,1:T(8,128)S(1)}, f32[32,2,512]{2,0,1:T(8,128)S(1)}, u32[]{:S(2)}, u32[]{:S(2)}) collective-permute-start(f32[32,2,512]{2,0,1:T(8,128)S(1)} %copy.94), channel_id=1, source_target_pairs={{4,0},{8,4},{12,8},{16,12},{20,16},{24,20},{28,24},{5,1},{9,5},{13... | collective-permute-start | bytes 393224 | tf_op jit(solution)/shard_map/ppermute | solution.py:24
  13.7 708.0 %all-reduce.2.cloned.1.call-start = ((), (), s32[]{:S(2)}) async-start(), calls=%async_computation | async-start | bytes 4194304 | tf_op jit(solution)/shard_map/psum | solution.py:93
  18.0 9.6 %copy-start.13 = (s32[2,8]{1,0:T(2,128)S(1)}, s32[2,8]{1,0:T(2,128)}, u32[]{:S(2)}) copy-start(s32[2,8]{1,0:T(2,128)} %param.13) | copy-start | bytes 196
  30.8 52.9 %collective-permute-start.3 = (f32[32,36,128]{2,0,1:T(8,128)S(1)}, f32[32,36,128]{2,0,1:T(8,128)S(1)}, u32[]{:S(2)}, u32[]{:S(2)}) collective-permute-start(f32[32,36,128]{2,0,1:T(8,128)S(1)} %get-tuple-element.14), channel_id=1, source_target_pairs={{1,0},{2,1},{3,2},{0,3},{5,4},{6,5},{7,6},{4,7},{9,8},{10,9},{11,1... | collective-permute-start | bytes 1769480 | tf_op jit(solution)/shard_map/ppermute | solution.py:24
  35.3 52.0 %collective-permute-start.2 = (f32[32,36,128]{2,0,1:T(8,128)S(1)}, f32[32,36,128]{2,0,1:T(8,128)S(1)}, u32[]{:S(2)}, u32[]{:S(2)}) collective-permute-start(f32[32,36,128]{2,0,1:T(8,128)S(1)} %get-tuple-element.13), channel_id=1, source_target_pairs={{0,1},{1,2},{2,3},{3,0},{4,5},{5,6},{6,7},{7,4},{8,9},{9,10},{10,1... | collective-permute-start | bytes 1769480 | tf_op jit(solution)/shard_map/ppermute | solution.py:22
  336.4 14.3 %copy-start.3 = (f32[16384,32]{1,0:T(8,128)S(1)}, f32[16384,32]{1,0:T(8,128)}, u32[]{:S(2)}) copy-start(f32[16384,32]{1,0:T(8,128)} %gather_fusion.3) | copy-start | bytes 6291460
  336.4 24.5 %slice-start = ((s8[8388608]{0:T(1024)(128)(4,1)}), s8[4194304]{0:T(1024)(128)(4,1)S(1)}, s32[]{:S(2)}) async-start(s8[8388608]{0:T(1024)(128)(4,1)} %bitcast.198), calls=%async_computation.2 | async-start | bytes 8388608
  350.7 10.2 %slice-start.1 = ((s8[8388608]{0:T(1024)(128)(4,1)}), s8[4194304]{0:T(1024)(128)(4,1)S(1)}, s32[]{:S(2)}) async-start(s8[8388608]{0:T(1024)(128)(4,1)} %bitcast.198), calls=%async_computation.3 | async-start | bytes 8388608
  350.7 10.2 %copy-start.7 = (pred[16384]{0:T(1024)(128)(4,1)S(1)}, pred[16384]{0:T(1024)(128)(4,1)}, u32[]{:S(2)}) copy-start(pred[16384]{0:T(1024)(128)(4,1)} %compare_and_fusion) | copy-start | bytes 49156
  624.3 3.0 copy-start.8
  624.3 3.0 copy-start.9
  624.3 3.0 copy-start.10
  624.3 3.0 copy-start.11
  627.3 2.2 copy-start.2
  634.5 0.7 copy-start.6
  674.3 47.4 %copy-start.12 = (pred[8]{0:T(512)(128)(4,1)S(1)}, pred[8]{0:T(512)(128)(4,1)}, u32[]{:S(2)}) copy-start(pred[8]{0:T(512)(128)(4,1)} %fusion.78) | copy-start | bytes 28
  674.3 54.3 %copy-start.1 = (s32[32,4]{0,1:T(4,128)S(1)}, s32[32,4]{0,1:T(4,128)}, u32[]{:S(2)}) copy-start(s32[32,4]{0,1:T(4,128)} %param.10) | copy-start | bytes 1540
Sparse Core Ops, SparseCore 0:
  13.8 75.6 all-gather.2
  634.7 86.9 all-reduce.1
where the time goes:
time: 739 us; the launch traced here: 735 us
  local copies, waits for them, and re-layouts  541 us (73%)
  waiting for transfers between devices  90.2 us (12%)
  other arithmetic  70.3 us (10%)
  between operations  13.9 us (2%)
  matrix products  11.9 us (2%)
  starting transfers between devices  8.32 us (1%)
    gather x12, local copies, waits for them, and re-layouts, take_cells(): return jnp.take(values, indices, axis=1)  250 us
    gather x4, local copies, waits for them, and re-layouts, stencil(): jnp.take(flat_field, (anchor + shift_by).reshape(-1), axis=1)  238 us
    select_n x4, other arithmetic, stencil(): jnp.take(flat_field, (anchor + shift_by).reshape(-1), axis=1)  47.7 us
    ppermute x2, waiting for transfers between devices, extended(): lax.ppermute(head, axis, [((i + 1) % count, i) for i in range(ends)])  45.2 us
    psum x1, waiting for transfers between devices, polar_work(): spectra = lax.psum(spectra, 'lon')  41.3 us
    reshape x4, local copies, waits for them, and re-layouts, stencil(): jnp.take(flat_field, (anchor + shift_by).reshape(-1), axis=1)  25.9 us
  transfers between devices with their start and end apart: 6, of which 3 were waited for; matrix products, arithmetic and copies ran while one was open for 48% of the time, Pallas kernels for 0%

commit v1 on v0

v1 whole, which is shorter than its diff:
```python
import functools
import math

import jax
import jax.numpy as jnp
import numpy as np
from jax import lax
from jax.experimental import pallas as pl
from jax.experimental.pallas import tpu as pltpu
from jax.sharding import PartitionSpec as P

NLON = 2048
BLK = 128
HL = 2
PROWS = 8
NBLK = NLON // BLK
SUB = 8
HALF = NBLK // 2 + 1
MESH = pl.DeviceIdType.MESH


def dft_tables():
    lanes = np.arange(BLK)
    angles = 2.0 * math.pi * (np.outer(lanes, lanes) % BLK) / BLK
    cosines, sines = np.cos(angles), np.sin(angles)
    matrix = np.block([[cosines, -sines], [sines, cosines]])
    turns = 2.0 * math.pi * np.outer(np.arange(NBLK), lanes) / NLON
    twiddle = np.stack([np.cos(turns), np.sin(turns)])
    return matrix.astype(np.float32), twiddle.astype(np.float32)


def add(left, right):
    if left is None:
        return right
    return left if right is None else left + right


def sub(left, right):
    if right is None:
        return left
    return -right if left is None else left - right


def scaled(value, factor):
    return None if value is None or factor == 0.0 else value * factor


def turned(value, cosine, sine):
    re, im = value
    cosine, sine = (0.0 if abs(v) < 1e-12 else v for v in (cosine, sine))
    if sine == 0.0 and cosine == 1.0:
        return value
    if cosine == 0.0 and abs(sine) == 1.0:
        if sine > 0:
            return (None if im is None else -im), re
        return im, (None if re is None else -re)
    return sub(scaled(re, cosine), scaled(im, sine)), add(scaled(re, sine), scaled(im, cosine))


def fourier(values, sign):
    count = len(values)
    if count == 1:
        return values
    even, odd = fourier(values[::2], sign), fourier(values[1::2], sign)
    low, high = [], []
    for k in range(count // 2):
        angle = sign * 2.0 * math.pi * k / count
        re, im = turned(odd[k], math.cos(angle), math.sin(angle))
        low.append((add(even[k][0], re), add(even[k][1], im)))
        high.append((sub(even[k][0], re), sub(even[k][1], im)))
    return low + high


def weights_of(t):
    return (
        -t * (t - 1.0) * (t - 2.0) / 6.0,
        (t + 1.0) * (t - 1.0) * (t - 2.0) / 2.0,
        -(t + 1.0) * t * (t - 2.0) / 2.0,
        (t + 1.0) * t * (t - 1.0) / 6.0,
    )


def wide(row):
    return jnp.broadcast_to(row, (SUB, BLK))


def lanes_at(values, index):
    return jnp.take_along_axis(values, index, axis=1, mode="promise_in_bounds")


def row_of(values, row):
    index = jnp.full((SUB, BLK), row, jnp.int32)
    return jnp.take_along_axis(values, index, axis=0, mode="promise_in_bounds")


def cubic_limited(values, anchor, weights):
    before = lanes_at(values, anchor - 1)
    here = lanes_at(values, anchor)
    after = lanes_at(values, anchor + 1)
    beyond = lanes_at(values, anchor + 2)
    mixed = weights[0] * before + weights[1] * here + weights[2] * after + weights[3] * beyond
    return jnp.minimum(jnp.maximum(mixed, jnp.minimum(here, after)), jnp.maximum(here, after))


def lanes(block):
    return pl.ds(pl.multiple_of(block * BLK, BLK), BLK)


def kernel(
    n_lat, n_lon, src_s, cut_s, trc, src_v, off, frac, mat, twd, out,
    mid, side, ring, ids, ids_out, fracs, ids_s, lim, spec, done, back,
    halo_send, halo_recv, pol_send, pol_recv, idx_send, idx_recv, frc_send, frc_recv,
    ret_send, ret_recv, loc_sem,
):
    channels, rows, cells = trc.shape
    nb = cells // BLK
    groups = channels // SUB
    shares = n_lon // groups
    work_rows = PROWS // shares
    tall = work_rows * SUB
    lat, lon = lax.axis_index("lat"), lax.axis_index("lon")
    first_row = lat * rows
    first_block = lon * nb
    right, left = lax.rem(lon + 1, n_lon), lax.rem(lon + n_lon - 1, n_lon)
    down, up = lax.rem(lat + 1, n_lat), lax.rem(lat + n_lat - 1, n_lat)
    polar = (lat == 0) | (lat == n_lat - 1)
    slab = jnp.where(lat == 0, 0, rows - PROWS)
    peers = [lax.rem(lon + d, n_lon) for d in range(1, n_lon)]

    barrier = pltpu.get_barrier_semaphore()
    for peer in peers:
        pl.semaphore_signal(barrier, inc=1, device_id=(lat, peer), device_id_type=MESH)
    for row in (up, down):
        for col in (left, lon, right):
            pl.semaphore_signal(barrier, inc=1, device_id=(row, col), device_id_type=MESH)

    @pl.loop(0, groups * (rows // SUB))
    def _(step):
        ch = pl.multiple_of(lax.rem(step, groups) * SUB, SUB)
        row = pl.multiple_of(lax.div(step, groups) * SUB, SUB)
        for b in range(nb):
            tile = trc[pl.ds(ch, SUB), pl.ds(row, SUB), b * BLK : (b + 1) * BLK]
            mid[pl.ds(HL + row, SUB), b, pl.ds(ch, SUB), :] = jnp.swapaxes(tile, 0, 1)

    pl.semaphore_wait(barrier, n_lon - 1 + 6)

    def group_of(place):
        return pl.multiple_of(lax.rem(place, groups) * SUB, SUB)

    def span_of(place):
        return pl.ds(place * nb, nb)

    def remote(src, dst, send, recv, device):
        return pltpu.make_async_remote_copy(
            src_ref=src, dst_ref=dst, send_sem=send, recv_sem=recv,
            device_id=device, device_id_type=MESH,
        )

    slab_at = pl.ds(pl.multiple_of(slab, SUB), PROWS)
    own = span_of(lon)
    ring_copies, back_copies = [], []
    for d, peer in enumerate(peers):
        ring_copies += [
            remote(ids_out, ids.at[lon], idx_send.at[d], idx_recv.at[d], (lat, peer)),
            remote(frac.at[slab_at], fracs.at[lon], frc_send.at[d], frc_recv.at[d], (lat, peer)),
            remote(
                mid.at[pl.ds(HL + slab, PROWS), :, pl.ds(group_of(peer), SUB), :],
                ring.at[:, own],
                pol_send.at[d], pol_recv.at[d], (lat, peer),
            ),
        ]
        back_copies.append(
            remote(
                done.at[:, span_of(peer)],
                back.at[
                    pl.ds(lax.div(lon, groups) * work_rows, work_rows), :, pl.ds(group_of(lon), SUB), :
                ],
                ret_send.at[d], ret_recv.at[d], (lat, peer),
            )
        )

    first, last = 0, nb - 1
    inner, top, bottom = pl.ds(HL, rows), pl.ds(HL, HL), pl.ds(rows, HL)
    over, under = pl.ds(0, HL), pl.ds(HL + rows, HL)
    plan = [
        (mid.at[bottom], mid.at[over], (down, lon)),
        (mid.at[top], mid.at[under], (up, lon)),
        (mid.at[inner, last], side.at[0, inner], (lat, right)),
        (mid.at[inner, first], side.at[1, inner], (lat, left)),
        (mid.at[bottom, last], side.at[0, over], (down, right)),
        (mid.at[bottom, first], side.at[1, over], (down, left)),
        (mid.at[top, last], side.at[0, under], (up, right)),
        (mid.at[top, first], side.at[1, under], (up, left)),
    ]
    halos = [
        remote(src, dst, halo_send.at[n], halo_recv.at[n], device)
        for n, (src, dst, device) in enumerate(plan)
    ]

    @pl.when(polar)
    def _():
        ids_out[0:PROWS] = off[slab_at]
        ids_out[PROWS : 2 * PROWS] = jnp.zeros((PROWS, cells), jnp.int32)
        ids_out[PROWS : 2 * PROWS, 0:nb] = src_v[slab_at]
        for copy in ring_copies:
            copy.start()

    for copy in halos:
        copy.start()

    def tile(group, b, edge):
        row = pl.multiple_of(group * SUB, SUB)
        at = lanes(b)
        weights = weights_of(frac[pl.ds(row, SUB), at])
        anchors = off[pl.ds(row, SUB), at]
        results = [[] for _ in range(groups)]
        for j in range(SUB):
            block_id = src_s[row + j, b]
            source_row = lax.div(block_id, NBLK) - first_row + HL
            source_row = jnp.clip(source_row, 0, rows + 2 * HL - 1)
            place = lax.rem(lax.rem(block_id, NBLK) - first_block + 1 + NBLK, NBLK)
            near = jnp.clip(place - 1, 0, nb - 1)
            far = jnp.minimum(place, 1)
            spot = jnp.full((SUB, BLK), place, jnp.int32)
            inside = (spot >= 1) & (spot <= nb)
            anchor = wide(anchors[j : j + 1])
            factors = [wide(w[j : j + 1]) for w in weights]
            for g in range(groups):
                chans = pl.ds(g * SUB, SUB)
                values = mid[source_row, near, chans, :]
                if edge:
                    values = jnp.where(inside, values, side[far, source_row, chans, :])
                results[g].append(cubic_limited(values, anchor, factors))
        for g in range(groups):
            out[g * SUB : (g + 1) * SUB, pl.ds(row, SUB), at] = jnp.swapaxes(
                jnp.stack(results[g]), 0, 1
            )

    tiles = rows // SUB

    def sweep(blocks, edge):
        count = len(blocks)
        if not count:
            return
        start, stride = blocks[0], (blocks[1] - blocks[0] if count > 1 else 1)

        @pl.loop(0, tiles * count)
        def _(step):
            group = lax.div(step, count)
            at_pole = ((lat == 0) & (group == 0)) | ((lat == n_lat - 1) & (group == tiles - 1))

            @pl.when(jnp.logical_not(at_pole))
            def _():
                tile(group, start + stride * lax.rem(step, count), edge)

    @pl.when(polar)
    def _():
        ids[lon] = ids_out[...]
        fracs[lon] = frac[slab_at]
        ring[:, own] = mid[pl.ds(HL + slab, PROWS), :, pl.ds(group_of(lon), SUB), :]
        for copy in ring_copies:
            copy.wait_recv()
        fetch = pltpu.make_async_copy(
            ids.at[:, pl.ds(PROWS, PROWS), pl.ds(0, BLK)], ids_s, loc_sem.at[0]
        )
        fetch.start()
        fetch.wait()
        row_base = lax.div(lon, groups) * work_rows
        slab_global = first_row + slab
        pole = jnp.where(lat == 0, 0, 1)

        @pl.loop(0, work_rows)
        def _(j):
            jw = row_base + j
            band = []
            for b in range(NBLK):
                q, bb = b // nb, b % nb
                block_id = ids_s[q, jw, bb]
                source_row = jnp.clip(lax.div(block_id, NBLK) - slab_global, 0, PROWS - 1)
                values = ring[source_row, lax.rem(block_id, NBLK)]
                at = pl.ds(bb * BLK, BLK)
                weights = weights_of(row_of(fracs[q, :, at], jw))
                anchor = row_of(ids[q, 0:PROWS, at], jw)
                limited = cubic_limited(values, anchor, weights)
                lim[j, b] = limited
                band.append((limited, None))
            waves = fourier(band, -1)
            for k in range(HALF):
                re, im = waves[k]
                cosine, sine = wide(twd[0, k : k + 1, :]), wide(twd[1, k : k + 1, :])
                at = pl.ds(pl.multiple_of(k * tall + j * SUB, SUB), SUB)
                if im is None:
                    spec[at, 0:BLK] = re * cosine
                    spec[at, BLK : 2 * BLK] = -re * sine
                else:
                    spec[at, 0:BLK] = re * cosine + im * sine
                    spec[at, BLK : 2 * BLK] = im * cosine - re * sine

        def transform():
            spec[...] = jnp.dot(
                spec[...], mat[...], precision=lax.Precision.HIGHEST,
                preferred_element_type=jnp.float32,
            )

        transform()

        @pl.loop(0, work_rows)
        def _(j):
            kappa = cut_s[pole, row_base + j].astype(jnp.float32)
            for k in range(HALF):
                wave = k + NBLK * lax.broadcasted_iota(jnp.int32, (SUB, BLK), 1)
                wave = jnp.minimum(wave, NLON - wave)
                kept = (wave >= 1) & (wave < NLON // 2)
                damping = 1.0 - kappa / jnp.maximum(wave, 1).astype(jnp.float32)
                damping = jnp.where(kept, jnp.maximum(damping, 0.0), 0.0) * (1.0 / NLON)
                at = pl.ds(pl.multiple_of(k * tall + j * SUB, SUB), SUB)
                spec[at, 0:BLK] = spec[at, 0:BLK] * damping
                spec[at, BLK : 2 * BLK] = -spec[at, BLK : 2 * BLK] * damping

        transform()

        @pl.loop(0, work_rows)
        def _(j):
            waves = []
            for k in range(HALF):
                at = pl.ds(pl.multiple_of(k * tall + j * SUB, SUB), SUB)
                re, im = spec[at, 0:BLK], spec[at, BLK : 2 * BLK]
                cosine, sine = wide(twd[0, k : k + 1, :]), wide(twd[1, k : k + 1, :])
                real = re * cosine + im * sine
                waves.append((real, None if k in (0, HALF - 1) else re * sine - im * cosine))
            for k in range(HALF, NBLK):
                re, im = waves[NBLK - k]
                waves.append((re, -im))
            removed = fourier(waves, 1)
            for b in range(NBLK):
                done[j, b] = lim[j, b] - removed[b][0]

        for copy in back_copies:
            copy.start()
        back[pl.ds(row_base, work_rows), :, pl.ds(group_of(lon), SUB), :] = done[:, own]

    for copy in halos[:2]:
        copy.wait_recv()
    sweep(list(range(1, nb - 1)), False)
    for copy in halos[2:]:
        copy.wait_recv()
    sweep(sorted({0, nb - 1}), True)

    @pl.when(polar)
    def _():
        for copy in back_copies:
            copy.wait_recv()

        @pl.loop(0, groups)
        def _(g):
            ch = pl.multiple_of(g * SUB, SUB)
            for b in range(nb):
                at = slice(b * BLK, (b + 1) * BLK)
                out[pl.ds(ch, SUB), slab_at, at] = jnp.swapaxes(back[:, b, pl.ds(ch, SUB), :], 0, 1)

        for copy in ring_copies + back_copies:
            copy.wait_send()

    for copy in halos:
        copy.wait_send()


def body(n_lat, n_lon, tracer, source, offset, fraction, cutoffs):
    channels, rows, cells = tracer.shape
    shares = n_lon // (channels // SUB)
    work_rows = PROWS // shares
    matrix, twiddle = dft_tables()
    dma = pltpu.SemaphoreType.DMA
    vmem, smem = pl.BlockSpec(memory_space=pltpu.VMEM), pl.BlockSpec(memory_space=pltpu.SMEM)
    return pl.pallas_call(
        functools.partial(kernel, n_lat, n_lon),
        out_shape=jax.ShapeDtypeStruct(tracer.shape, jnp.float32),
        in_specs=[smem, smem] + [vmem] * 6,
        out_specs=vmem,
        scratch_shapes=[
            pltpu.VMEM((rows + 2 * HL, cells // BLK, channels, BLK), jnp.float32),
            pltpu.VMEM((2, rows + 2 * HL, channels, BLK), jnp.float32),
            pltpu.VMEM((PROWS, NBLK, SUB, BLK), jnp.float32),
            pltpu.VMEM((n_lon, 2 * PROWS, cells), jnp.int32),
            pltpu.VMEM((2 * PROWS, cells), jnp.int32),
            pltpu.VMEM((n_lon, PROWS, cells), jnp.float32),
            pltpu.SMEM((n_lon, PROWS, BLK), jnp.int32),
            pltpu.VMEM((work_rows, NBLK, SUB, BLK), jnp.float32),
            pltpu.VMEM((HALF * work_rows * SUB, 2 * BLK), jnp.float32),
            pltpu.VMEM((work_rows, NBLK, SUB, BLK), jnp.float32),
            pltpu.VMEM((PROWS, cells // BLK, channels, BLK), jnp.float32),
            dma((8,)), dma((8,)),
        ] + [dma((n_lon - 1,))] * 8 + [dma((1,))],
        compiler_params=pltpu.CompilerParams(
            collective_id=0, has_side_effects=True, vmem_limit_bytes=40 * 2**20
        ),
        cost_estimate=pl.CostEstimate(flops=10**9, bytes_accessed=5 * 10**6, transcendentals=0),
    )(source, cutoffs, tracer, source, offset, fraction, jnp.asarray(matrix), jnp.asarray(twiddle))


def solution(mesh):
    placed = (P(None, "lat", "lon"), P("lat", "lon"), P("lat", "lon"), P("lat", "lon"), P())
    step = functools.partial(body, mesh.shape["lat"], mesh.shape["lon"])
    return jax.shard_map(
        step, mesh=mesh, in_specs=placed, out_specs=P(None, "lat", "lon"), check_vma=False
    )
```

time: 739 us -> 54.2 us (0.07)
  local copies, waits for them, and re-layouts: 541 us -> 7.7 us
  waiting for transfers between devices: 90.2 us -> 0 us
  other arithmetic: 70.3 us -> 0 us
  Pallas kernels: 0 us -> 46.1 us
  between operations: 13.9 us -> 0.02 us
  matrix products: 11.9 us -> 0 us
  starting transfers between devices: 8.32 us -> 0 us
    gather x18 -> x0, local copies, waits for them, and re-layouts: 489 us -> none  [the longest x12 250 us: take_cells(): return jnp.take(values, indices, axis=1)]
    ppermute x4 -> x0, waiting for transfers between devices: 48.8 us -> none  [the longest x2 45.2 us: extended(): lax.ppermute(head, axis, [((i + 1) % count, i) for i in range(ends)])]
    select_n x5 -> x0, other arithmetic: 47.7 us -> none  [the longest x4 47.7 us: stencil(): jnp.take(flat_field, (anchor + shift_by).reshape(-1), axis=1)]
    pallas_call x0 -> x1, Pallas kernels: none -> 46.1 us  [body(): pl.pallas_call(functools.partial(kernel, n_lat, n_lon), out_shape=jax.Sha...]
    psum x1 -> x0, waiting for transfers between devices: 41.3 us -> none  [polar_work(): spectra = lax.psum(spectra, 'lon')]
    reshape x4 -> x0, local copies, waits for them, and re-layouts: 25.9 us -> none  [stencil(): jnp.take(flat_field, (anchor + shift_by).reshape(-1), axis=1)]
    dot_general x2 -> x0, matrix products: 11.9 us -> none  [the longest x1 6.86 us: polar_work(): jnp.einsum('pcrk,xk->pcrx', spectra * weights[:, None], fourier_basis, pr...]
    cos x1 -> x0, other arithmetic: 9.57 us -> none  [spectral_table(): return jnp.concatenate([jnp.cos(angles), jnp.sin(angles)], axis=1)]
  transfers between devices with their start and end apart: 6 -> 0, of which waited for: 3 -> 0; matrix products, arithmetic and copies ran while one was open for 48% -> 0% of each run, Pallas kernels for 0% -> 0%
where the time goes in v1:
time: 54.2 us; the launch traced here: 53.8 us
  Pallas kernels  46.1 us (85%)
  local copies, waits for them, and re-layouts  7.7 us (14%)
    pallas_call x1, Pallas kernels, body(): pl.pallas_call(functools.partial(kernel, n_lat, n_lon), out_shape=jax.Sha...  46.1 us
    unnamed x14, local copies, waits for them, and re-layouts  7.7 us

profile of v1, /device:TPU:0, one launch (start us, length us, event | category | flops | bytes accessed | tf_op | source)
XLA Modules:
  0.0 53.8 jit_solution(1053476467676628656)
XLA Ops:
  0.0 0.8 %copy.8.src_s.src_v = s32[32,4]{1,0:T(8,128)S(1)} copy(s32[32,4]{0,1:T(4,128)} %param.8) | data formatting | bytes 1024 | tf_op args[1]
  0.8 0.0 copy-start
  0.8 1.6 %copy-done = f32[32,32,512]{2,1,0:T(8,128)S(1)} copy-done((f32[32,32,512]{2,1,0:T(8,128)S(1)}, f32[32,32,512]{2,1,0:T(8,128)}, u32[]{:S(2)}) %copy-start) | copy-done | bytes 2097176
  2.4 0.0 copy-start.1
  2.4 0.9 %copy-done.1 = f32[256,256]{1,0:T(8,128)S(1)} copy-done((f32[256,256]{1,0:T(8,128)S(1)}, f32[256,256]{1,0:T(8,128)}, u32[]{:S(2)}) %copy-start.1) | copy-done | bytes 262168
  3.3 0.0 copy-start.2
  3.3 0.8 %copy-done.2 = s32[32,512]{1,0:T(8,128)S(1)} copy-done((s32[32,512]{1,0:T(8,128)S(1)}, s32[32,512]{1,0:T(8,128)}, u32[]{:S(2)}) %copy-start.2) | copy-done | bytes 65560
  4.1 0.0 copy-start.3
  4.1 0.8 %copy-done.3 = f32[32,512]{1,0:T(8,128)S(1)} copy-done((f32[32,512]{1,0:T(8,128)S(1)}, f32[32,512]{1,0:T(8,128)}, u32[]{:S(2)}) %copy-start.3) | copy-done | bytes 65560
  5.0 0.0 copy-start.4
  5.0 0.7 %copy-done.4 = f32[2,16,128]{2,1,0:T(8,128)S(1)} copy-done((f32[2,16,128]{2,1,0:T(8,128)S(1)}, f32[2,16,128]{2,1,0:T(8,128)}, u32[]{:S(2)}) %copy-start.4) | copy-done | bytes 16408
  5.7 0.0 copy-start.5
  5.7 0.7 %copy-done.5 = s32[2,8]{1,0:T(2,128)S(1)} copy-done((s32[2,8]{1,0:T(2,128)S(1)}, s32[2,8]{1,0:T(2,128)}, u32[]{:S(2)}) %copy-start.5) | copy-done | bytes 88
  6.4 46.1 %shard_map.73 = f32[32,32,512]{2,1,0:T(8,128)S(1)} custom-call(s32[32,4]{1,0:T(8,128)S(1)} %copy.8.src_s.src_v, s32[2,8]{1,0:T(2,128)S(1)} %copy-done.5, f32[32,32,512]{2,1,0:T(8,128)S(1)} %copy-done, s32[32,4]{1,0:T(8,128)S(1)} %copy.8.src_s.src_v, s32[32,512]{1,0:T(8,128)S(1)} %copy-done.2, f32[32,512]{1,0:T(8,128)S(1)} %copy-done.3, ...), custom_call_target="tpu_custom_call" | custom-call | flops 1000000000 | bytes 5000000 | tf_op jit(solution)/shard_map/pallas_call | solution.py:375
  52.5 1.3 %copy.11 = f32[32,32,512]{2,1,0:T(8,128)} copy(f32[32,32,512]{2,1,0:T(8,128)S(1)} %shard_map.73) | data formatting | bytes 4194304
Async XLA Ops:
  0.8 1.6 %copy-start = (f32[32,32,512]{2,1,0:T(8,128)S(1)}, f32[32,32,512]{2,1,0:T(8,128)}, u32[]{:S(2)}) copy-start(f32[32,32,512]{2,1,0:T(8,128)} %trc.1) | copy-start | bytes 6291460
  2.4 0.9 %copy-start.1 = (f32[256,256]{1,0:T(8,128)S(1)}, f32[256,256]{1,0:T(8,128)}, u32[]{:S(2)}) copy-start(f32[256,256]{1,0:T(8,128)} %constant.4.clone.mat) | copy-start | bytes 786436
  3.3 0.8 %copy-start.2 = (s32[32,512]{1,0:T(8,128)S(1)}, s32[32,512]{1,0:T(8,128)}, u32[]{:S(2)}) copy-start(s32[32,512]{1,0:T(8,128)} %off.1) | copy-start | bytes 196612
  4.1 0.8 %copy-start.3 = (f32[32,512]{1,0:T(8,128)S(1)}, f32[32,512]{1,0:T(8,128)}, u32[]{:S(2)}) copy-start(f32[32,512]{1,0:T(8,128)} %frac.1) | copy-start | bytes 196612
  5.0 0.7 %copy-start.4 = (f32[2,16,128]{2,1,0:T(8,128)S(1)}, f32[2,16,128]{2,1,0:T(8,128)}, u32[]{:S(2)}) copy-start(f32[2,16,128]{2,1,0:T(8,128)} %constant.5.clone.twd) | copy-start | bytes 49156
  5.7 0.7 %copy-start.5 = (s32[2,8]{1,0:T(2,128)S(1)}, s32[2,8]{1,0:T(2,128)}, u32[]{:S(2)}) copy-start(s32[2,8]{1,0:T(2,128)} %cut_s.1) | copy-start | bytes 196
